TPU v7x, 512 devices: a whole 4x4x16 slice. The times are simulated.
512 devices in a mesh: chan: 64 (over z, y), rad: 8 (over x, core).
Axes of the slice: x: 4, y: 4, z: 16, core: 2. Of those that a mesh axis runs over, the one named last changes fastest.
Arguments:
- trial_block: float32 [1024, 16, 128], P('chan', None, 'rad')
- ham_blocks: bfloat16 [1024, 8, 128, 128], P('chan', None, 'rad'), may hold values from -0.1875 to 0.1875
- partners: int32 [1024, 8], P('chan'), may hold values from 0 to 1023, as said below
- stored_at: int32 [1024], replicated, may hold values from 0 to 1023, as said below
- precond_diag: float32 [1024, 128], P('chan', 'rad'), may hold values from 1 to 10
Outputs:
- new_block: float32 [1024, 16, 128], P('chan', None, 'rad')
- ritz_values: float32 [16], replicated
Inputs may be any that keep to these rules, and one draw needn't show every extreme that they name: `stored_at`: A permutation of the channel numbers. `partners`: among the 128 entries of the rows p with p // 16 = d, for every d, at most 4 have stored_at[partner] // 16 equal to any one value; for every d some value has exactly 4.
All inputs are finite; a program needn't handle non-finite values.
Results may differ from a plain program's by a relative error of at most 0.0051.
Values may be sent and summed in bfloat16 or wider, within the bound.
A program may use at most 64 MiB of HBM per device.

v0:
```python
import jax
import jax.numpy as jnp
from jax import lax
from jax.sharding import PartitionSpec as P

NCH = 1024
NB = 128


def chol_solve(factor, rhs):
    first = lax.linalg.triangular_solve(factor, rhs, left_side=True, lower=True)
    return lax.linalg.triangular_solve(factor, first, left_side=True, lower=True, transpose_a=True)


def inner_products(left, right):
    return jnp.einsum("pkr,plr->kl", left, right, precision=lax.Precision.HIGHEST)


def body(trial_block, ham_blocks, partners, stored_at, precond_diag):
    n_chan = lax.axis_size("chan")
    ch_dev = trial_block.shape[0]
    vectors = trial_block.shape[1]
    ncoup = partners.shape[1]
    capacity = 2 * ch_dev * ncoup // n_chan
    stored_rows = jnp.take(stored_at, partners.reshape(-1))
    owner_dev = stored_rows // ch_dev
    local_row = stored_rows % ch_dev
    one_hot = (owner_dev[:, None] == jnp.arange(n_chan, dtype=jnp.int32)[None, :]).astype(jnp.int32)
    running = jnp.cumsum(one_hot, axis=0)
    order_rank = jnp.sum(running * one_hot, axis=1) - 1
    slot_index = owner_dev * capacity + order_rank
    wanted = (
        jnp.zeros((n_chan * capacity,), jnp.int32)
        .at[slot_index]
        .set(local_row)
        .reshape(n_chan, capacity)
    )
    asked = lax.all_to_all(wanted, "chan", split_axis=0, concat_axis=0, tiled=True)
    rounded = trial_block.astype(jnp.bfloat16)
    whole_rows = lax.all_gather(rounded, "rad", axis=2, tiled=True)
    served = whole_rows[asked]
    received = lax.all_to_all(served, "chan", split_axis=0, concat_axis=0, tiled=True)
    full_splines = received.shape[3]
    coupled = received.reshape(n_chan * capacity, vectors, full_splines)[slot_index]
    coupled = coupled.reshape(ch_dev, ncoup, vectors, full_splines)
    applied = lax.dot_general(
        coupled, ham_blocks, (((1, 3), (1, 3)), ((0,), (0,))), preferred_element_type=jnp.float32
    )
    total_rows = jnp.float32(NCH * NB)
    proj_a, proj_b = lax.psum(
        (inner_products(trial_block, applied), inner_products(trial_block, trial_block)),
        ("chan", "rad"),
    )
    factor = jnp.linalg.cholesky(proj_b)
    coefficients = chol_solve(factor, proj_a)
    ritz_values = jnp.diagonal(coefficients)
    residual = applied - jnp.einsum(
        "pkr,kl->plr", trial_block, coefficients, precision=lax.Precision.HIGHEST
    )
    correction = residual / precond_diag[:, None, :]
    correlation = lax.psum(inner_products(trial_block, correction), ("chan", "rad"))
    mixing = chol_solve(factor, correlation)
    projected = correction - jnp.einsum(
        "pkr,kl->plr", trial_block, mixing, precision=lax.Precision.HIGHEST
    )
    correlation_gram = lax.psum(inner_products(projected, projected), ("chan", "rad")) / total_rows
    gram_factor = jnp.linalg.cholesky(correlation_gram)
    local_splines = projected.shape[2]
    flat_rows = jnp.transpose(projected, (1, 0, 2)).reshape(vectors, -1)
    solved = lax.linalg.triangular_solve(gram_factor, flat_rows, left_side=True, lower=True)
    new_block = jnp.transpose(solved.reshape(vectors, ch_dev, local_splines), (1, 0, 2))
    return (new_block, ritz_values)


def solution(mesh):
    return jax.shard_map(
        body,
        mesh=mesh,
        in_specs=(
            P("chan", None, "rad"),
            P("chan", None, "rad", None),
            P("chan", None),
            P(),
            P("chan", "rad"),
        ),
        out_specs=(P("chan", None, "rad"), P()),
        check_vma=False,
    )
```

profile of v0, /device:TPU:1, one launch (start us, length us, event | category | flops | bytes accessed | tf_op | source)
XLA Modules:
  0.0 426.4 jit_solution(2646082566353192529)
XLA Ops:
  0.6 0.0 copy-start
  0.6 0.8 copy.36
  1.5 0.1 reshape.211
  1.5 0.1 reshape.212
  1.6 0.0 copy-start.1
  1.7 0.7 copy-done.1
  2.3 1.0 gather_fusion
  3.3 0.1 fusion.4
  3.4 0.0 copy-start.2
  3.4 0.2 reduce_window_sum.11
  3.6 0.2 select_reduce_fusion
  3.8 1.0 scatter_custom_fusion
  4.8 0.7 all_to_all.11
  5.5 19.3 %all-to-all-start = ((s32[64,1,4]{2,1,0:T(1,128)}), s32[64,1,4]{2,1,0:T(1,128)S(1)}, u32[]{:S(2)}, u32[]{:S(2)}) async-start(s32[64,1,4]{2,1,0:T(1,128)} %bitcast.4), calls=%async_computation | async-start | bytes 65536 | tf_op jit(solution)/shard_map/all_to_all | solution.py:38
  24.8 0.0 copy-done.2
  24.8 0.1 copy.35
  24.9 14.3 %all_gather.3 = bf16[16,16,128]{1,0,2:T(8,128)(2,1)S(1)} all-gather(bf16[16,16,16]{1,0,2:T(8,128)(2,1)S(1)} %copy.35), channel_id=1, replica_groups=mesh['chan'=64,'rad'=8] {'rad'}, dimensions={2}, use_global_device_ids=true | all-gather | bytes 73728 | tf_op jit(solution)/shard_map/all_gather | solution.py:40
  39.2 0.4 copy.39
  39.6 0.0 all-to-all-done
  39.6 0.1 reshape.230
  39.8 1.8 gather_fusion.1
  41.5 14.8 %all-to-all-start.1 = ((bf16[64,4,16,128]{3,2,1,0:T(8,128)(2,1)}), bf16[64,4,16,128]{3,2,1,0:T(8,128)(2,1)S(1)}, u32[]{:S(2)}, u32[]{:S(2)}) async-start(bf16[64,4,16,128]{3,2,1,0:T(8,128)(2,1)} %bitcast.6), calls=%async_computation.1 | async-start | bytes 2097152 | tf_op jit(solution)/shard_map/all_to_all | solution.py:42
  56.4 0.2 convolution_bitcast_fusion.5
  56.6 52.5 %all-to-all-done.1 = bf16[64,4,16,128]{3,2,1,0:T(8,128)(2,1)S(1)} async-done(((bf16[64,4,16,128]{3,2,1,0:T(8,128)(2,1)}), bf16[64,4,16,128]{3,2,1,0:T(8,128)(2,1)S(1)}, u32[]{:S(2)}, u32[]{:S(2)}) %all-to-all-start.1) | async-done | bytes 1048608 | tf_op jit(solution)/shard_map/all_to_all | solution.py:42
  109.2 0.7 gather_fusion.2
  109.9 0.0 copy-done
  109.9 0.3 fusion.27
  110.2 0.3 convolution_bitcast_fusion.4
  110.4 103.4 %all-reduce = (f32[16,16]{0,1:T(8,128)S(1)}, f32[16,16]{0,1:T(8,128)S(1)}) all-reduce(f32[16,16]{0,1:T(8,128)S(1)} %convolution_bitcast_fusion.4, f32[16,16]{0,1:T(8,128)S(1)} %convolution_bitcast_fusion.5), channel_id=1, replica_groups=mesh['chan'=64,'rad'=8] {'chan','rad'}, use_global_device_ids=true, to_apply=%region_6.8 | all-reduce | flops 512 | bytes 4096 | tf_op jit(solution)/shard_map/psum | solution.py:50
  213.8 0.1 copy.41
  213.9 1.5 cholesky.44
  215.4 0.6 compare_reduce_fusion.1
  216.0 0.6 fusion.5
  216.7 1.2 custom-call.17
  217.9 0.2 fusion.14
  218.1 0.1 fusion.16
  218.3 0.0 copy-start.3
  218.3 0.3 fusion.9
  218.6 0.4 copy-done.3
  219.0 0.3 convolution_bitcast_fusion.3
  219.3 99.6 %psum.30 = f32[16,16]{0,1:T(8,128)S(1)} all-reduce(f32[16,16]{0,1:T(8,128)S(1)} %convolution_bitcast_fusion.3), channel_id=1, replica_groups=mesh['chan'=64,'rad'=8] {'chan','rad'}, use_global_device_ids=true, to_apply=%region_7.11 | all-reduce | flops 256 | bytes 2048 | tf_op jit(solution)/shard_map/psum | solution.py:61
  318.9 0.2 fusion.11
  319.1 0.2 convolution_bitcast_fusion.2
  319.3 0.3 fusion.1
  319.6 0.3 convolution_bitcast_fusion.1
  319.8 99.4 %psum.31 = f32[16,16]{0,1:T(8,128)S(1)} all-reduce(f32[16,16]{0,1:T(8,128)S(1)} %convolution_bitcast_fusion.1), channel_id=1, replica_groups=mesh['chan'=64,'rad'=8] {'chan','rad'}, use_global_device_ids=true, to_apply=%region_8.12 | all-reduce | flops 256 | bytes 2048 | tf_op jit(solution)/shard_map/psum | solution.py:66
  419.2 0.1 copy.44
  419.2 1.5 cholesky.55
  420.7 0.6 compare_reduce_fusion
  421.4 0.6 fusion.6
  422.0 1.2 custom-call.11
  423.3 0.1 copy.45
  423.3 0.1 reshape.215
  423.4 0.1 copy.56
  423.5 1.2 gather_fusion.3
  424.7 1.7 convolution_bitcast_fusion
  (14 shorter events, 0.2 us)
Async XLA Ops:
  0.6 109.2 %copy-start = (bf16[16,8,16,128]{3,2,1,0:T(8,128)(2,1)S(1)}, bf16[16,8,16,128]{3,2,1,0:T(8,128)(2,1)}, u32[]{:S(2)}) copy-start(bf16[16,8,16,128]{3,2,1,0:T(8,128)(2,1)} %param.11) | copy-start | bytes 1572868
  1.6 0.7 copy-start.1
  3.4 21.4 %copy-start.2 = (f32[16,16,16]{2,1,0:T(8,128)S(1)}, f32[16,16,16]{2,1,0:T(8,128)}, u32[]{:S(2)}) copy-start(f32[16,16,16]{2,1,0:T(8,128)} %param.10) | copy-start | bytes 49156
  5.5 34.1 %all-to-all-start = ((s32[64,1,4]{2,1,0:T(1,128)}), s32[64,1,4]{2,1,0:T(1,128)S(1)}, u32[]{:S(2)}, u32[]{:S(2)}) async-start(s32[64,1,4]{2,1,0:T(1,128)} %bitcast.4), calls=%async_computation | async-start | bytes 65536 | tf_op jit(solution)/shard_map/all_to_all | solution.py:38
  41.5 67.6 %all-to-all-start.1 = ((bf16[64,4,16,128]{3,2,1,0:T(8,128)(2,1)}), bf16[64,4,16,128]{3,2,1,0:T(8,128)(2,1)S(1)}, u32[]{:S(2)}, u32[]{:S(2)}) async-start(bf16[64,4,16,128]{3,2,1,0:T(8,128)(2,1)} %bitcast.6), calls=%async_computation.1 | async-start | bytes 2097152 | tf_op jit(solution)/shard_map/all_to_all | solution.py:42
  218.3 0.7 copy-start.3
where the time goes:
time: 427 us; the launch traced here: 426 us
  blocking collectives  317 us (74%)
  waiting for transfers between devices  52.5 us (12%)
  starting transfers between devices  34.1 us (8%)
  local copies, waits for them, and re-layouts  9.41 us (2%)
  other arithmetic  8.53 us (2%)
  matrix products  4.37 us (1%)
    psum x1, blocking collectives, body(): lax.psum((inner_products(trial_block, applied), inner_products(trial_bloc...  103 us
    psum x1, blocking collectives, body(): lax.psum(inner_products(trial_block, correction), ('chan', 'rad'))  99.6 us
    psum x1, blocking collectives, body(): lax.psum(inner_products(projected, projected), ('chan', 'rad')) / total_rows  99.4 us
    all_to_all x1, waiting for transfers between devices, body(): lax.all_to_all(served, 'chan', split_axis=0, concat_axis=0, tiled=True)  52.5 us
    all_to_all x1, starting transfers between devices, body(): lax.all_to_all(wanted, 'chan', split_axis=0, concat_axis=0, tiled=True)  19.3 us
    all_to_all x1, starting transfers between devices, body(): lax.all_to_all(served, 'chan', split_axis=0, concat_axis=0, tiled=True)  14.8 us
    all_gather x1, blocking collectives, body(): whole_rows = lax.all_gather(rounded, 'rad', axis=2, tiled=True)  14.3 us
  transfers between devices with their start and end apart: 2, of which 1 were waited for; matrix products, arithmetic and copies ran while one was open for 0% of the time, Pallas kernels for 0%

commit v1 on v0

--- a/solution.py
+++ b/solution.py
@@ -58,7 +58,7 @@
         "pkr,kl->plr", trial_block, coefficients, precision=lax.Precision.HIGHEST
     )
     correction = residual / precond_diag[:, None, :]
-    correlation = lax.psum(inner_products(trial_block, correction), ("chan", "rad"))
+    correlation = lax.psum(lax.psum(inner_products(trial_block, correction), "rad"), "chan")
     mixing = chol_solve(factor, correlation)
     projected = correction - jnp.einsum(
         "pkr,kl->plr", trial_block, mixing, precision=lax.Precision.HIGHEST

time: 427 us -> 481 us (1.13)
  blocking collectives: 317 us -> 371 us
    psum x1 -> x2, blocking collectives: 99.6 us -> 128 us  [the longest x1 116 us: body(): lax.psum(lax.psum(inner_products(trial_block, correction), 'rad'), 'chan')]
    psum x1, blocking collectives: 99.4 us -> 124 us  [body(): lax.psum(inner_products(projected, projected), ('chan', 'rad')) / total_rows]
where the time goes in v1:
time: 481 us; the launch traced here: 480 us
  blocking collectives  371 us (77%)
  waiting for transfers between devices  52.5 us (11%)
  starting transfers between devices  34.1 us (7%)
  local copies, waits for them, and re-layouts  9.41 us (2%)
  other arithmetic  8.53 us (2%)
    psum x1, blocking collectives, body(): lax.psum(inner_products(projected, projected), ('chan', 'rad')) / total_rows  124 us
    psum x1, blocking collectives, body(): lax.psum(lax.psum(inner_products(trial_block, correction), 'rad'), 'chan')  116 us
    psum x1, blocking collectives, body(): lax.psum((inner_products(trial_block, applied), inner_products(trial_bloc...  103 us
    all_to_all x1, waiting for transfers between devices, body(): lax.all_to_all(served, 'chan', split_axis=0, concat_axis=0, tiled=True)  52.5 us
    all_to_all x1, starting transfers between devices, body(): lax.all_to_all(wanted, 'chan', split_axis=0, concat_axis=0, tiled=True)  19.3 us
    all_to_all x1, starting transfers between devices, body(): lax.all_to_all(served, 'chan', split_axis=0, concat_axis=0, tiled=True)  14.8 us
    all_gather x1, blocking collectives, body(): whole_rows = lax.all_gather(rounded, 'rad', axis=2, tiled=True)  14.3 us
    psum x1, blocking collectives, body(): lax.psum(inner_products(trial_block, correction), 'rad')  12.7 us
  transfers between devices with their start and end apart: 2, of which 1 were waited for; matrix products, arithmetic and copies ran while one was open for 0% of the time, Pallas kernels for 0%

profile of v1, /device:TPU:1, one launch (start us, length us, event | category | flops | bytes accessed | tf_op | source)
XLA Modules:
  0.0 480.3 jit_solution(1064263090432129403)
XLA Ops:
  0.6 0.0 copy-start
  0.6 0.8 copy.36
  1.5 0.1 reshape.211
  1.5 0.1 reshape.212
  1.6 0.0 copy-start.1
  1.7 0.7 copy-done.1
  2.3 1.0 gather_fusion
  3.3 0.1 fusion.4
  3.4 0.0 copy-start.2
  3.4 0.2 reduce_window_sum.11
  3.6 0.2 select_reduce_fusion
  3.8 1.0 scatter_custom_fusion
  4.8 0.7 all_to_all.11
  5.5 19.3 %all-to-all-start = ((s32[64,1,4]{2,1,0:T(1,128)}), s32[64,1,4]{2,1,0:T(1,128)S(1)}, u32[]{:S(2)}, u32[]{:S(2)}) async-start(s32[64,1,4]{2,1,0:T(1,128)} %bitcast.4), calls=%async_computation | async-start | bytes 65536 | tf_op jit(solution)/shard_map/all_to_all | solution.py:38
  24.8 0.0 copy-done.2
  24.8 0.1 copy.35
  24.9 14.3 %all_gather.3 = bf16[16,16,128]{1,0,2:T(8,128)(2,1)S(1)} all-gather(bf16[16,16,16]{1,0,2:T(8,128)(2,1)S(1)} %copy.35), channel_id=1, replica_groups=mesh['chan'=64,'rad'=8] {'rad'}, dimensions={2}, use_global_device_ids=true | all-gather | bytes 73728 | tf_op jit(solution)/shard_map/all_gather | solution.py:40
  39.2 0.4 copy.39
  39.6 0.0 all-to-all-done
  39.6 0.1 reshape.230
  39.8 1.8 gather_fusion.1
  41.5 14.8 %all-to-all-start.1 = ((bf16[64,4,16,128]{3,2,1,0:T(8,128)(2,1)}), bf16[64,4,16,128]{3,2,1,0:T(8,128)(2,1)S(1)}, u32[]{:S(2)}, u32[]{:S(2)}) async-start(bf16[64,4,16,128]{3,2,1,0:T(8,128)(2,1)} %bitcast.6), calls=%async_computation.1 | async-start | bytes 2097152 | tf_op jit(solution)/shard_map/all_to_all | solution.py:42
  56.4 0.2 convolution_bitcast_fusion.5
  56.6 52.5 %all-to-all-done.1 = bf16[64,4,16,128]{3,2,1,0:T(8,128)(2,1)S(1)} async-done(((bf16[64,4,16,128]{3,2,1,0:T(8,128)(2,1)}), bf16[64,4,16,128]{3,2,1,0:T(8,128)(2,1)S(1)}, u32[]{:S(2)}, u32[]{:S(2)}) %all-to-all-start.1) | async-done | bytes 1048608 | tf_op jit(solution)/shard_map/all_to_all | solution.py:42
  109.2 0.7 gather_fusion.2
  109.9 0.0 copy-done
  109.9 0.3 fusion.27
  110.2 0.3 convolution_bitcast_fusion.4
  110.4 103.4 %all-reduce = (f32[16,16]{0,1:T(8,128)S(1)}, f32[16,16]{0,1:T(8,128)S(1)}) all-reduce(f32[16,16]{0,1:T(8,128)S(1)} %convolution_bitcast_fusion.4, f32[16,16]{0,1:T(8,128)S(1)} %convolution_bitcast_fusion.5), channel_id=1, replica_groups=mesh['chan'=64,'rad'=8] {'chan','rad'}, use_global_device_ids=true, to_apply=%region_6.8 | all-reduce | flops 512 | bytes 4096 | tf_op jit(solution)/shard_map/psum | solution.py:50
  213.8 0.1 copy.41
  213.9 1.5 cholesky.44
  215.4 0.6 compare_reduce_fusion.1
  216.0 0.6 fusion.5
  216.7 1.2 custom-call.17
  217.9 0.2 fusion.14
  218.1 0.1 fusion.16
  218.3 0.0 copy-start.3
  218.3 0.3 fusion.9
  218.6 0.4 copy-done.3
  219.0 0.3 convolution_bitcast_fusion.3
  219.3 12.7 %psum.37 = f32[16,16]{0,1:T(8,128)S(1)} all-reduce(f32[16,16]{0,1:T(8,128)S(1)} %convolution_bitcast_fusion.3), channel_id=1, replica_groups=mesh['chan'=64,'rad'=8] {'rad'}, use_global_device_ids=true, to_apply=%region_7.11 | all-reduce | flops 256 | bytes 2048 | tf_op jit(solution)/shard_map/psum | solution.py:61
  232.0 115.7 %psum.38 = f32[16,16]{0,1:T(8,128)S(1)} all-reduce(f32[16,16]{0,1:T(8,128)S(1)} %psum.37), channel_id=1, replica_groups=mesh['chan'=64,'rad'=8] {'chan'}, use_global_device_ids=true, to_apply=%region_8.12 | all-reduce | flops 256 | bytes 2048 | tf_op jit(solution)/shard_map/psum | solution.py:61
  347.7 0.2 fusion.11
  347.9 0.2 convolution_bitcast_fusion.2
  348.1 0.3 fusion.1
  348.4 0.3 convolution_bitcast_fusion.1
  348.6 124.5 %psum.39 = f32[16,16]{0,1:T(8,128)S(1)} all-reduce(f32[16,16]{0,1:T(8,128)S(1)} %convolution_bitcast_fusion.1), channel_id=1, replica_groups=mesh['chan'=64,'rad'=8] {'chan','rad'}, use_global_device_ids=true, to_apply=%region_9.13 | all-reduce | flops 256 | bytes 2048 | tf_op jit(solution)/shard_map/psum | solution.py:66
  473.1 0.1 copy.44
  473.2 1.5 cholesky.55
  474.6 0.6 compare_reduce_fusion
  475.3 0.6 fusion.6
  475.9 1.2 custom-call.11
  477.2 0.1 copy.45
  477.2 0.1 reshape.215
  477.3 0.1 copy.56
  477.4 1.2 gather_fusion.3
  478.6 1.7 convolution_bitcast_fusion
  (14 shorter events, 0.2 us)
Async XLA Ops:
  0.6 109.2 %copy-start = (bf16[16,8,16,128]{3,2,1,0:T(8,128)(2,1)S(1)}, bf16[16,8,16,128]{3,2,1,0:T(8,128)(2,1)}, u32[]{:S(2)}) copy-start(bf16[16,8,16,128]{3,2,1,0:T(8,128)(2,1)} %param.11) | copy-start | bytes 1572868
  1.6 0.7 copy-start.1
  3.4 21.4 %copy-start.2 = (f32[16,16,16]{2,1,0:T(8,128)S(1)}, f32[16,16,16]{2,1,0:T(8,128)}, u32[]{:S(2)}) copy-start(f32[16,16,16]{2,1,0:T(8,128)} %param.10) | copy-start | bytes 49156
  5.5 34.1 %all-to-all-start = ((s32[64,1,4]{2,1,0:T(1,128)}), s32[64,1,4]{2,1,0:T(1,128)S(1)}, u32[]{:S(2)}, u32[]{:S(2)}) async-start(s32[64,1,4]{2,1,0:T(1,128)} %bitcast.4), calls=%async_computation | async-start | bytes 65536 | tf_op jit(solution)/shard_map/all_to_all | solution.py:38
  41.5 67.6 %all-to-all-start.1 = ((bf16[64,4,16,128]{3,2,1,0:T(8,128)(2,1)}), bf16[64,4,16,128]{3,2,1,0:T(8,128)(2,1)S(1)}, u32[]{:S(2)}, u32[]{:S(2)}) async-start(bf16[64,4,16,128]{3,2,1,0:T(8,128)(2,1)} %bitcast.6), calls=%async_computation.1 | async-start | bytes 2097152 | tf_op jit(solution)/shard_map/all_to_all | solution.py:42
  218.3 0.7 copy-start.3
